TPU v7x, 256 devices: a whole 4x4x8 slice. The times are simulated.
256 devices in a mesh: blk: 128 (over z, x, y), rep: 2 (over core).
Axes of the slice: x: 4, y: 4, z: 8, core: 2. Of those that a mesh axis runs over, the one named last changes fastest.
Arguments:
- right_side: float32 [8, 262144], P(None, 'blk'), may hold values from -6 to 6
- coords: float32 [3, 262144], P(None, 'blk'), as said below
- counts: int32 [512], P('blk'), may hold values from 128 to 512
- pair_list: int32 [3, 2560], P(None, ('blk', 'rep')), may hold values from 0 to 511, as said below
Outputs:
- solution: float32 [8, 262144], P(None, 'blk')
- residual: float32 [8, 262144], P(None, 'blk')
Inputs may be any that keep to these rules, and one draw needn't show every extreme that they name: `pair_list`: row 0 holds a row block, row 1 a partner block from the row block to 4 blocks after it, row 2 is 1 for a live pair and 0 for an empty slot. The live pairs are exactly the block pairs, each once with the lower block as row block, whose locations can lie closer than 4; all other block pairs have every distance 4 or more. The blocks of group g, 4 g to 4 g + 3, own slots 2 * 10 g onwards, 20 of them, live pairs first; an empty slot names the group's first block twice. Some row block has a partner exactly 4 blocks after it. `coords`: each block's locations lie in a slab along the first coordinate, blocks in increasing order without gaps; second and third coordinates between 0 and 1.
All inputs are finite; a program needn't handle non-finite values.
Results may differ from a plain program's by a relative error of at most 0.0003.
Values sent between devices are 32-bit elements; how exact they have to be, the bound alone decides.
A program may use at most 64 MiB of HBM per device.

v0:
```python
import math

import jax
import jax.numpy as jnp
from jax import lax
from jax.sharding import PartitionSpec as P

ITERS = 2
SPAN = 4


sill_factor = 0.1
range_factor = 0.5
nugget = 0.5
highest = lax.Precision.HIGHEST


def shifted(x, axis, by):
    peers = lax.axis_size(axis)
    pairs = [(i, i + by) for i in range(peers) if 0 <= i + by < peers]
    return lax.ppermute(x, axis, pairs)


def cov_tile(left, right, left_alive, right_alive, taper_radius):
    diff = left[:, :, None] - right[:, None, :]
    dist = jnp.sqrt(jnp.sum(diff * diff, axis=0))
    scaled = dist * (math.sqrt(3.0) / (range_factor * taper_radius))
    matern = (1.0 + scaled) * jnp.exp(-scaled)
    ratio = dist / taper_radius
    taper = jnp.maximum(1.0 - ratio, 0.0)
    taper = taper * taper * taper * taper * (1.0 + 4.0 * ratio)
    return sill_factor / taper_radius * matern * taper * left_alive[:, None] * right_alive[None, :]


def add_block(accum, term, where):
    current = lax.dynamic_index_in_dim(accum, where, 1, keepdims=False)
    return lax.dynamic_update_index_in_dim(accum, current + term, where, 1)


def pair_apply(
    accum, row_block, col_block, row_weight, col_weight, probes, blocks, alive, taper_radius
):
    left = lax.dynamic_index_in_dim(blocks, row_block, 1, keepdims=False)
    right = lax.dynamic_index_in_dim(blocks, col_block, 1, keepdims=False)
    left_alive = lax.dynamic_index_in_dim(alive, row_block, 0, keepdims=False)
    right_alive = lax.dynamic_index_in_dim(alive, col_block, 0, keepdims=False)
    kernel = cov_tile(left, right, left_alive, right_alive, taper_radius)
    vec_col = lax.dynamic_index_in_dim(probes, col_block, 1, keepdims=False)
    vec_row = lax.dynamic_index_in_dim(probes, row_block, 1, keepdims=False)
    to_row = (
        lax.dot_general(vec_col, kernel, (((1,), (1,)), ((), ())), precision=highest) * row_weight
    )
    to_col = jnp.dot(vec_row, kernel, precision=highest) * col_weight
    accum = add_block(accum, to_row, row_block)
    return add_block(accum, to_col, col_block)


def inner_products(first, second):
    return lax.dot_general(first, second, (((1,), (1,)), ((), ())), precision=highest)


def solve_small(matrix, rhs):
    factor = jnp.linalg.cholesky(matrix)
    return jax.scipy.linalg.cho_solve((factor, True), rhs)


def squares_sum(residual):
    return lax.psum(inner_products(residual, residual), "blk")


def on_device(right_side, coords, counts, pair_list):
    block_count = counts.shape[0]
    tile_len = coords.shape[1] // block_count
    probe_count = right_side.shape[0]
    taper_radius = float(SPAN)
    alive = (lax.broadcasted_iota(jnp.int32, (block_count, tile_len), 1) < counts[:, None]).astype(
        jnp.float32
    )
    flat_alive = alive.reshape(block_count * tile_len)
    first_block = lax.axis_index("blk") * block_count
    next_coords, next_alive = shifted((coords, flat_alive), "blk", -1)
    own_rows = pair_list[0]
    own_cols = pair_list[1]
    own_flag = pair_list[2].astype(jnp.float32)
    field_coords = jnp.concatenate([coords, next_coords], axis=1).reshape(
        3, 2 * block_count, tile_len
    )
    field_alive = jnp.concatenate([flat_alive, next_alive]).reshape(2 * block_count, tile_len)
    row_ids = own_rows - first_block
    col_ids = own_cols - first_block
    col_weights = own_flag * (own_rows != own_cols).astype(jnp.float32)
    slot_count = row_ids.shape[0]
    residual = right_side * flat_alive
    direction = residual
    solution = jnp.zeros_like(residual)
    norm_now = squares_sum(residual)
    for iteration in range(ITERS):
        near_probes = shifted(direction, "blk", -1)
        joined = jnp.concatenate([direction, near_probes], axis=1)
        field_probes = joined.reshape(probe_count, 2 * block_count, tile_len)

        def slot_body(slot_index, accum):
            return pair_apply(
                accum,
                row_ids[slot_index],
                col_ids[slot_index],
                own_flag[slot_index],
                col_weights[slot_index],
                field_probes,
                field_coords,
                field_alive,
                taper_radius,
            )

        apply_accum = lax.fori_loop(
            0, slot_count, slot_body, jnp.zeros(field_probes.shape, jnp.float32)
        )
        spilled = apply_accum[:, block_count:].reshape(probe_count, block_count * tile_len)
        received = shifted(spilled, "blk", 1)
        own_part = (
            apply_accum[:, :block_count].reshape(probe_count, block_count * tile_len) + received
        )
        image = lax.psum(own_part, "rep") + nugget * direction
        curvature = lax.psum(inner_products(direction, image), "blk")
        alpha = solve_small(curvature, norm_now)
        solution = solution + jnp.dot(alpha.T, direction, precision=highest)
        residual = residual - jnp.dot(alpha.T, image, precision=highest)
        if iteration + 1 < ITERS:
            norm_next = squares_sum(residual)
            beta = solve_small(norm_now, norm_next)
            direction = residual + jnp.dot(beta.T, direction, precision=highest)
            norm_now = norm_next
    return (solution, residual)


def solution(mesh):
    placed = (P(None, "blk"), P(None, "blk"), P("blk"), P(None, ("blk", "rep")))
    return jax.shard_map(
        on_device,
        mesh=mesh,
        in_specs=placed,
        out_specs=(P(None, "blk"), P(None, "blk")),
        check_vma=False,
    )
```

profile of v0, /device:TPU:0, one launch (start us, length us, event | category | flops | bytes accessed | tf_op | source)
XLA Modules:
  0.0 1381.9 jit_solution(10695356167187175767)
XLA Ops:
  14.3 1.8 collective-permute-done.1
  16.9 1.9 collective-permute-done
  18.9 105.6 %while.30 = (s32[]{:T(128)}, f32[8,8,512]{2,0,1:T(8,128)S(1)}, s32[10]{0:T(128)S(1)}, s32[10]{0:T(128)S(1)}, f32[8,8,512]{2,1,0:T(8,128)S(1)}, /*index=5*/f32[3,...) while((s32[]{:T(128)}, f32[8,8,512]{2,0,1:T(8,128)S(1)}, ...), condition=%wide.region_2.3_spmd, body=%wide.region_0.2_spmd.sunk | while | flops 56639496 | bytes 5521697 | solution.py:115
  26.6 1.6 fusion.106
  37.1 1.6 fusion.106
  47.7 1.6 fusion.106
  58.3 1.6 fusion.106
  68.8 1.6 fusion.106
  79.4 1.6 fusion.106
  89.9 1.6 fusion.106
  100.5 1.6 fusion.106
  111.1 1.6 fusion.106
  124.6 3.9 collective-permute-start.3
  128.5 1.9 collective-permute-done.3
  131.3 36.1 %all-reduce.4.cloned.1.call-done = f32[8,2048]{1,0:T(8,128)} async-done(((f32[8,2048]{1,0:T(8,128)}), f32[8,2048]{1,0:T(8,128)}) %all-reduce.4.cloned.1.call-update) | async-done | bytes 65552 | tf_op jit(solution)/shard_map/psum | solution.py:123
  168.4 353.7 %all-reduce = (f32[8,8]{0,1:T(8,128)S(1)}, f32[8,8]{0,1:T(8,128)S(1)}) all-reduce(f32[8,8]{0,1:T(8,128)S(1)} %fusion.60, f32[8,8]{0,1:T(8,128)S(1)} %fusion.28), channel_id=1, replica_groups=mesh['blk'=128,'rep'=2] {'blk'}, use_global_device_ids=true, to_apply=%region_7.9 | all-reduce | flops 128 | bytes 1024 | tf_op jit(solution)/shard_map/psum | solution.py:68
  529.2 342.2 %psum.45 = f32[8,8]{1,0:T(8,128)S(1)} all-reduce(f32[8,8]{1,0:T(8,128)S(1)} %fusion.62), channel_id=1, replica_groups=mesh['blk'=128,'rep'=2] {'blk'}, use_global_device_ids=true, to_apply=%region_8.11 | all-reduce | flops 64 | bytes 512 | tf_op jit(solution)/shard_map/psum | solution.py:68
  873.3 4.9 collective-permute-done.4
  878.3 105.6 %while.31 = (s32[]{:T(128)}, f32[8,8,512]{2,0,1:T(8,128)S(1)}, s32[10]{0:T(128)S(1)}, s32[10]{0:T(128)S(1)}, f32[8,8,512]{2,1,0:T(8,128)S(1)}, /*index=5*/f32[3,...) while((s32[]{:T(128)}, f32[8,8,512]{2,0,1:T(8,128)S(1)}, ...), condition=%wide.region_11.14_spmd, body=%wide.region_9.13_spmd.sunk | while | flops 56639496 | bytes 5521697 | solution.py:115
  886.0 1.6 fusion.113
  907.1 1.6 fusion.113
  928.2 1.6 fusion.113
  938.8 1.6 fusion.113
  949.4 1.6 fusion.113
  959.9 1.6 fusion.113
  970.5 1.6 fusion.113
  981.0 1.6 fusion.113
  984.0 3.9 collective-permute-start.5
  987.9 1.9 collective-permute-done.5
  990.7 28.1 %all-reduce.6.cloned.1.call-done = f32[8,2048]{1,0:T(8,128)} async-done(((f32[8,2048]{1,0:T(8,128)}), f32[8,2048]{1,0:T(8,128)}) %all-reduce.6.cloned.1.call-update) | async-done | bytes 65552 | tf_op jit(solution)/shard_map/psum | solution.py:123
  1019.8 349.6 %psum.47 = f32[8,8]{0,1:T(8,128)S(1)} all-reduce(f32[8,8]{0,1:T(8,128)S(1)} %fusion.29), channel_id=1, replica_groups=mesh['blk'=128,'rep'=2] {'blk'}, use_global_device_ids=true, to_apply=%region_13.16 | all-reduce | flops 64 | bytes 512 | tf_op jit(solution)/shard_map/psum | solution.py:124
  1373.4 1.7 convolution_subtract_fusion
  (304 shorter events, 130.1 us)
Async XLA Ops:
  7.2 160.2 %all-reduce.4.cloned.1.call-start = ((), (), s32[]{:S(2)}) async-start(), calls=%async_computation | async-start | bytes 131072 | tf_op jit(solution)/shard_map/psum | solution.py:123
  7.9 6.3 collective-permute-start.2
  9.2 6.9 collective-permute-start.1
  11.4 7.4 collective-permute-start
  124.6 5.8 collective-permute-start.3
  131.1 887.7 %all-reduce.6.cloned.1.call-start = ((), (), s32[]{:S(2)}) async-start(), calls=%async_computation.1 | async-start | bytes 131072 | tf_op jit(solution)/shard_map/psum | solution.py:123
  872.0 6.2 collective-permute-start.4
  984.0 5.8 collective-permute-start.5
Sparse Core Ops, SparseCore 0:
  131.2 36.1 all-reduce.3
  990.5 28.1 all-reduce.5
where the time goes:
time: 1380 us
  blocking collectives  1050 us (76%)
  loops' own time  78.8 us (6%)
  waiting for transfers between devices  76.5 us (6%)
  matrix products  65.9 us (5%)
  local copies, waits for them, and re-layouts  50.3 us (4%)
  other arithmetic  37.6 us (3%)
  between operations  14.2 us (1%)
    psum x2, blocking collectives, squares_sum(): return lax.psum(inner_products(residual, residual), 'blk')  696 us
    psum x1, blocking collectives, on_device(): curvature = lax.psum(inner_products(direction, image), 'blk')  350 us
    another operation x2, loops' own time, on_device(): lax.fori_loop(0, slot_count, slot_body, jnp.zeros(field_probes.shape, jnp...  78.8 us
    psum x2, waiting for transfers between devices, on_device(): image = lax.psum(own_part, 'rep') + nugget * direction  64.1 us
    dot_general x20, matrix products, pair_apply(): lax.dot_general(vec_col, kernel, (((1,), (1,)), ((), ())), precision=high...  32.2 us
  transfers between devices with their start and end apart: 8, of which 7 were waited for; matrix products, arithmetic and copies ran while one was open for 0% of the time, Pallas kernels for 0%

commit v1 on v0

v1 whole, which is shorter than its diff:
```python
import functools
import math

import jax
import jax.numpy as jnp
from jax import lax
from jax.experimental import pallas as pl
from jax.experimental.pallas import tpu as pltpu
from jax.sharding import PartitionSpec as P

SPAN = 4
BLOCKS = 4
SLOTS = 512
PROBES = 8
FAR = 5

sill = 0.1 / SPAN
nugget = 0.5
level = nugget + sill

KAPPA = math.sqrt(3.0) / (0.5 * SPAN) * math.log2(math.e)
REACH = SPAN * KAPPA
MATERN_ROOT = math.log2(math.e)
TAPER_ROOT = KAPPA * SPAN / 4.0
UNIT = REACH**4 * 2.0**REACH * MATERN_ROOT * TAPER_ROOT

PAIRS = [(i, j) for i in range(BLOCKS) for j in range(i + 1)]
CHUNK = 16
CHUNKS = SLOTS // CHUNK
XROW = 32

f32 = jnp.float32
bf16 = jnp.bfloat16
MESH = pl.DeviceIdType.MESH
HIGHEST = lax.Precision.HIGHEST
NT = (((1,), (1,)), ((), ()))


def split(x, parts):
    out = []
    for _ in range(parts - 1):
        piece = x.astype(bf16).astype(f32)
        out.append(piece)
        x = x - piece
    out.append(x.astype(bf16).astype(f32))
    return out


def two_parts(x):
    high = x.astype(bf16)
    low = (x - high.astype(f32)).astype(bf16)
    return jnp.concatenate([high, low], axis=0)


def mm(a, b):
    return jnp.dot(a, b, precision=HIGHEST, preferred_element_type=f32)


def inverse(matrix):
    rows = lax.broadcasted_iota(jnp.int32, (PROBES, PROBES), 0)
    eye = (rows == lax.broadcasted_iota(jnp.int32, (PROBES, PROBES), 1)).astype(f32)
    return eliminate(matrix, eye)


def eliminate(matrix, rhs):
    work = jnp.concatenate([matrix, rhs], axis=1)
    rows = lax.broadcasted_iota(jnp.int32, work.shape, 0)
    for k in range(PROBES):
        pivot = work[k : k + 1, k : k + 1]
        scaled = work[k : k + 1, :] / pivot
        column = jnp.broadcast_to(work[:, k : k + 1], work.shape)
        work = jnp.where(rows == k, scaled, work - column * scaled)
    return work[:, PROBES:]


def kernel(
    groups,
    plane,
    rs_ref,
    co_ref,
    cnt_ref,
    sol_ref,
    res_ref,
    cnt,
    co,
    geo_s,
    geo_r,
    qq,
    qc,
    alive,
    lraw,
    xc,
    lfeat,
    rraw,
    rfeat,
    xr,
    vrow,
    vcol,
    kc,
    yzs,
    tr,
    tc,
    mine,
    spill,
    other_in,
    spill_in,
    ahead_in,
    tile,
    sums_a,
    tile_b,
    sums_b,
    local_sem,
    geo_send,
    geo_recv,
    q_send,
    q_recv,
    mine_send,
    spill_send,
    other_recv,
    spill_recv,
    ahead_recv,
    red_send,
    red_recv,
):
    g = lax.axis_index("blk")
    c = lax.axis_index("rep")
    nxt = lax.rem(g + 1, groups)
    prv = lax.rem(g + groups - 1, groups)
    zs = groups // plane
    z, inplane = g // plane, lax.rem(g, plane)
    ring = zs * 2
    place = z * 2 + c

    def in_plane(k):
        return {"blk": z * plane + lax.rem(inplane + k, plane), "rep": c}

    def across(k):
        at = lax.rem(place + k, ring)
        return {"blk": (at // 2) * plane + inplane, "rep": lax.rem(at, 2)}

    barrier = pltpu.get_barrier_semaphore()

    def greet_plane(k, carry):
        pl.semaphore_signal(barrier, inc=1, device_id=in_plane(k), device_id_type=MESH)
        return carry

    def greet_across(k, carry):
        pl.semaphore_signal(barrier, inc=1, device_id=across(k), device_id_type=MESH)
        return carry

    for near in (prv, nxt):
        for core in (0, 1):
            pl.semaphore_signal(
                barrier, inc=1, device_id={"blk": near, "rep": core}, device_id_type=MESH
            )
    lax.fori_loop(1, plane, greet_plane, 0)
    lax.fori_loop(1, ring, greet_across, 0)

    loads = [
        pltpu.make_async_copy(cnt_ref, cnt, local_sem.at[0]),
        pltpu.make_async_copy(co_ref, co, local_sem.at[1]),
    ]
    for b in range(BLOCKS):
        loads.append(
            pltpu.make_async_copy(
                rs_ref.at[:, pl.ds(b * SLOTS, SLOTS)], qq.at[b, 0:PROBES], local_sem.at[2 + b]
            )
        )
    for load in loads:
        load.start()
    for load in loads:
        load.wait()

    slot = lax.broadcasted_iota(jnp.int32, (1, SLOTS), 1)
    for b in range(BLOCKS):
        live = (slot < cnt[b]).astype(f32)
        alive[0, b] = live
        geo_s[b // 2, (b % 2) * 4 : (b % 2) * 4 + 3] = co[:, b * SLOTS : (b + 1) * SLOTS]
        geo_s[b // 2, (b % 2) * 4 + 3 : (b % 2) * 4 + 4] = live
        qq[b, 0:PROBES] = qq[b, 0:PROBES] * live

    pl.semaphore_wait(barrier, 4 + plane - 1 + ring - 1)

    back = {"blk": prv, "rep": 1}
    geo_copy = pltpu.make_async_remote_copy(
        src_ref=geo_s.at[c],
        dst_ref=geo_r.at[c],
        send_sem=geo_send,
        recv_sem=geo_recv.at[c],
        device_id=back,
        device_id_type=MESH,
    )
    geo_copy.start()
    q_copies = []
    for h in range(2):
        copy = pltpu.make_async_remote_copy(
            src_ref=qq.at[2 * h + c, 0:PROBES],
            dst_ref=qc.at[2 * h + c, 0:PROBES],
            send_sem=q_send.at[h],
            recv_sem=q_recv.at[2 * h + c],
            device_id=back,
            device_id_type=MESH,
        )
        copy.start()
        q_copies.append(copy)

    origin = geo_s[0, 0:1, 0:1]

    def features(geo, b):
        r = (b % 2) * 4
        x = (geo[b // 2, r : r + 1] - origin) * KAPPA
        y = (geo[b // 2, r + 1 : r + 2] - 0.5) * KAPPA
        w = (geo[b // 2, r + 2 : r + 3] - 0.5) * KAPPA
        return x, split(y, 3), split(w, 3), split(y * y + w * w, 3)

    ones = jnp.ones((1, SLOTS), f32)
    lraw[...] = jnp.zeros_like(lraw)
    rraw[...] = jnp.zeros_like(rraw)
    for b in range(BLOCKS):
        x, ys, ws, ns = features(geo_s, b)
        rows = []
        for q in (ys, ws):
            rows += [-2.0 * q[k] for k in (0, 0, 1, 1, 0, 2)]
        rows += ns + [ones] * 3
        for k, row in enumerate(rows):
            lraw[b, k : k + 1] = row
        lraw[b, XROW : XROW + 1] = x
        turned = lraw[b].T
        xc[b] = turned
        lfeat[b] = turned.astype(bf16)
        vrow[b] = two_parts(qq[b, 0:PROBES])

    @pl.when(c == 0)
    def _():
        for h in range(2):
            geo_r[h] = geo_s[h]
        for b in range(BLOCKS):
            qc[b, 0:PROBES] = qq[b, 0:PROBES]

    @pl.when(c == 1)
    def _():
        for h in range(2):
            pltpu.make_async_copy(geo_s.at[h], geo_r.at[h], geo_recv.at[h]).wait()

    for b in range(BLOCKS):
        x, ys, ws, ns = features(geo_r, b)
        rows = []
        for q in (ys, ws):
            rows += [q[k] for k in (0, 1, 0, 1, 2, 0)]
        rows += [ones] * 3 + ns
        for k, row in enumerate(rows):
            rraw[b, k : k + 1] = row
        rfeat[b] = rraw[b].astype(bf16)
        xr[b] = x
        alive[1, b] = geo_r[b // 2, (b % 2) * 4 + 3 : (b % 2) * 4 + 4]

    def build(n, chunk):
        i, j = PAIRS[n]
        s = pl.ds(chunk * CHUNK, CHUNK)
        along = xc[i, s, XROW : XROW + 1] - xr[j]
        square = jnp.maximum(along * along + yzs[n % 2, s], 1e-12)
        dist = square * lax.rsqrt(square)
        inside = jnp.maximum(REACH - dist, 0.0)
        decay = jnp.exp2(inside)
        twice = inside * inside
        value = (twice * twice) * decay * ((dist + MATERN_ROOT) * (dist + TAPER_ROOT))
        high = value.astype(bf16)
        kc[n, s, 0:SLOTS] = high
        kc[n, s, SLOTS:] = (value - high.astype(f32)).astype(bf16)

    def across_part(n, quarter):
        i, j = PAIRS[n]
        s = pl.ds(quarter * 128, 128)
        yzs[n % 2, s] = jnp.dot(lfeat[i, s], rfeat[j], preferred_element_type=f32)

    mirror = jnp.where(c == 0, 0.0, 1.0).astype(f32)

    def apply(n, quarter, it):
        i, j = PAIRS[n]
        h = quarter % 2
        s = pl.ds(h * 256, 256)
        if quarter < 2:
            both = jnp.dot(vrow[i][:, h * 256 : h * 256 + 256], kc[n, s], preferred_element_type=f32)
            both = both[:, :SLOTS] + both[:, SLOTS:]
            part = both[:PROBES] + both[PROBES:]
            if i == j:
                part = part * mirror
            tc[it, j] += part
        else:
            both = lax.dot_general(vcol[j], kc[n, s, 0:SLOTS], NT, preferred_element_type=f32)
            both += lax.dot_general(vcol[j], kc[n, s, SLOTS:], NT, preferred_element_type=f32)
            tr[it, i, :, h * 256 : h * 256 + 256] += both[:PROBES] + both[PROBES:]

    tr[...] = jnp.zeros_like(tr)
    tc[...] = jnp.zeros_like(tc)

    sends = []

    def send_block(b, it):
        mine[it, b] = tr[it, b] + (1.0 - mirror) * tc[it, b]

        def copy(src, dst, send_sem, recv_sem, blk, rep):
            return pltpu.make_async_remote_copy(
                src_ref=src,
                dst_ref=dst,
                send_sem=send_sem,
                recv_sem=recv_sem,
                device_id={"blk": blk, "rep": rep},
                device_id_type=MESH,
            )

        first = copy(
            mine.at[it, b], other_in.at[it, b], mine_send.at[0, it, b], other_recv.at[it, b], g, 1 - c
        )
        first.start()
        sends.append(first)
        if it == 0:
            second = copy(
                mine.at[it, b], ahead_in.at[c, b], mine_send.at[1, it, b], ahead_recv.at[c, b], prv, 1
            )
            second.start()
            sends.append(second)

        @pl.when(c == 1)
        def _():
            for core in range(2):
                copy(
                    tc.at[it, b],
                    spill_in.at[it, b],
                    spill_send.at[core, it, b],
                    spill_recv.at[it, b],
                    nxt,
                    core,
                ).start()

    def wait_for(dst, sem):
        pltpu.make_async_copy(mine.at[0, 0], dst, sem).wait()

    def gather_block(b, it):
        wait_for(other_in.at[it, b], other_recv.at[it, b])
        wait_for(spill_in.at[it, b], spill_recv.at[it, b])
        total = (mine[it, b] + other_in[it, b]) + spill_in[it, b]
        old = qq[b, it * PROBES : (it + 1) * PROBES]
        qq[b, (it + 1) * PROBES : (it + 2) * PROBES] = total * (alive[0, b] * (1.0 / UNIT)) - old

    def gather_ahead(b):
        @pl.when(c == 0)
        def _():
            qc[b, PROBES:] = qq[b, PROBES : 2 * PROBES]

        @pl.when(c == 1)
        def _():
            for core in range(2):
                wait_for(ahead_in.at[core, b], ahead_recv.at[core, b])
            total = (ahead_in[0, b] + ahead_in[1, b]) + tc[0, b]
            qc[b, PROBES:] = total * (alive[1, b] * (1.0 / UNIT)) - qc[b, 0:PROBES]

    for quarter in range(4):
        across_part(0, quarter)

    @pl.when(c == 1)
    def _():
        for b in range(BLOCKS):
            wait_for(qc.at[b, 0:PROBES], q_recv.at[b])

    for b in range(BLOCKS):
        vcol[b] = two_parts(qc[b, 0:PROBES])

    last = len(PAIRS) - 1
    for n in range(len(PAIRS)):
        for chunk in range(CHUNKS):
            build(n, chunk)
            if chunk % 8 == 3 and n < last:
                across_part(n + 1, chunk // 8)
            if chunk % 8 == 7 and n > 0:
                apply(n - 1, chunk // 8, 0)
        if n > 0 and PAIRS[n - 1][0] == BLOCKS - 1:
            send_block(PAIRS[n - 1][1], 0)
    for quarter in range(4):
        apply(last, quarter, 0)
    send_block(BLOCKS - 1, 0)

    for n, (i, j) in enumerate(PAIRS):
        if j == 0:
            gather_block(i, 0)
            gather_ahead(i)
            vrow[i] = two_parts(qq[i, PROBES : 2 * PROBES])
            vcol[i] = two_parts(qc[i, PROBES:])
        for quarter in range(4):
            apply(n, quarter, 1)
        if i == BLOCKS - 1:
            send_block(j, 1)

    tile[...] = jnp.zeros_like(tile)

    @pl.when(c == 0)
    def _():
        gram = jnp.zeros((2 * PROBES, 2 * PROBES), f32)
        for b in range(BLOCKS):
            pair = qq[b, 0 : 2 * PROBES]
            gram += lax.dot_general(pair, pair, NT, precision=HIGHEST, preferred_element_type=f32)
        tile[:, 0:16] = gram[0:PROBES]
        tile[:, 16:32] = gram[PROBES:]

    part = jnp.zeros((PROBES, PROBES), f32)
    for b in range(BLOCKS):
        part += lax.dot_general(
            qq[b, PROBES : 2 * PROBES], tr[1, b], NT, precision=HIGHEST, preferred_element_type=f32
        )
        part += lax.dot_general(
            qc[b, PROBES:], tc[1, b], NT, precision=HIGHEST, preferred_element_type=f32
        )
    tile[:, 32:40] = part * (1.0 / UNIT)

    def spread(src, dst, me, count, target, k):
        def send(step, carry):
            pltpu.make_async_remote_copy(
                src_ref=src,
                dst_ref=dst.at[me],
                send_sem=red_send.at[k],
                recv_sem=red_recv.at[k],
                device_id=target(step),
                device_id_type=MESH,
            ).start()
            return carry

        lax.fori_loop(1, count, send, 0)
        dst[me] = src[...]
        everything = dst.at[pl.ds(0, count - 1)]
        pltpu.make_async_copy(everything, everything, red_recv.at[k]).wait()
        total = dst[0]
        for at in range(1, count):
            total = total + dst[at]
        return total

    tile_b[...] = spread(tile, sums_a, inplane, plane, in_plane, 0)
    sums = spread(tile_b, sums_b, place, ring, across, 1)

    for b in range(BLOCKS):
        gather_block(b, 1)

    h00, h01, h11 = sums[:, 0:8], sums[:, 8:16], sums[:, 24:32]
    h12 = sums[:, 32:40] - h11
    curv_inv = inverse(level * h00 + sill * h01)
    alpha = mm(curv_inv, h00)
    m2 = mm(curv_inv, h01)
    m1 = mm(curv_inv, h11)
    alpha_t = mm(h00, curv_inv)
    w_t = sill * mm(h01, curv_inv)
    n_fwd = sill * (mm(h00, m1) - mm(h01, m2))
    n_t = sill * (mm(h11, alpha) - mm(h01, m2))
    beta = sill * mm(curv_inv, n_t)
    beta_t = sill * mm(n_fwd, curv_inv)
    new = mm(h00, beta)
    f_fwd = sill * m2 + beta
    f_t = w_t + beta_t
    curv = level * new - sill * mm(n_fwd, f_fwd)
    curv += sill**3 * mm(mm(alpha_t, h12) - mm(h01, m1), alpha)
    both = mm(new, eliminate(curv, jnp.concatenate([f_t, sill * alpha_t], axis=1)))
    x_t, y_t = both[:, :PROBES], both[:, PROBES:]
    zero = jnp.zeros((PROBES, PROBES), f32)
    top = jnp.concatenate([alpha_t + x_t, -y_t, zero], axis=1)
    low = jnp.concatenate(
        [w_t - level * x_t, level * y_t - sill * x_t - sill * alpha_t, sill * y_t], axis=1
    )
    weights = jnp.concatenate([top, low], axis=0)
    for b in range(BLOCKS):
        result = mm(weights, qq[b])
        sol_ref[:, b * SLOTS : (b + 1) * SLOTS] = result[:PROBES]
        res_ref[:, b * SLOTS : (b + 1) * SLOTS] = result[PROBES:]

    geo_copy.wait_send()
    for copy in q_copies:
        copy.wait_send()
    for copy in sends:
        copy.wait_send()

    @pl.when(c == 1)
    def _():
        for it in range(2):
            for b in range(BLOCKS):
                for core in range(2):
                    pltpu.make_async_copy(
                        tc.at[it, b], spill.at[b], spill_send.at[core, it, b]
                    ).wait()

    for k, (dst, count) in enumerate(((sums_a, plane), (sums_b, ring))):
        everything = dst.at[pl.ds(0, count - 1)]
        pltpu.make_async_copy(everything, everything, red_send.at[k]).wait()


def on_device(groups, plane, right_side, coords, counts, pair_list):
    del pair_list
    ring = groups // plane * 2
    block = (BLOCKS, PROBES, SLOTS)
    dma = pltpu.SemaphoreType.DMA
    width = right_side.shape[1]
    shape = jax.ShapeDtypeStruct((PROBES, width), f32)
    anywhere = pl.BlockSpec(memory_space=pl.ANY)
    vmem = pl.BlockSpec(memory_space=pltpu.VMEM)
    return pl.pallas_call(
        functools.partial(kernel, groups, plane),
        out_shape=(shape, shape),
        in_specs=[anywhere] * 3,
        out_specs=(vmem, vmem),
        scratch_shapes=[
            pltpu.SMEM((BLOCKS,), jnp.int32),
            pltpu.VMEM((3, width), f32),
            pltpu.VMEM((2, 8, SLOTS), f32),
            pltpu.VMEM((2, 8, SLOTS), f32),
            pltpu.VMEM((BLOCKS, 3 * PROBES, SLOTS), f32),
            pltpu.VMEM((BLOCKS, 2 * PROBES, SLOTS), f32),
            pltpu.VMEM((2, BLOCKS, 1, SLOTS), f32),
            pltpu.VMEM((BLOCKS, 128, SLOTS), f32),
            pltpu.VMEM((BLOCKS, SLOTS, 128), f32),
            pltpu.VMEM((BLOCKS, SLOTS, 128), bf16),
            pltpu.VMEM((BLOCKS, 128, SLOTS), f32),
            pltpu.VMEM((BLOCKS, 128, SLOTS), bf16),
            pltpu.VMEM((BLOCKS, 1, SLOTS), f32),
            pltpu.VMEM((BLOCKS, 2 * PROBES, SLOTS), bf16),
            pltpu.VMEM((BLOCKS, 2 * PROBES, SLOTS), bf16),
            pltpu.VMEM((len(PAIRS), SLOTS, 2 * SLOTS), bf16),
            pltpu.VMEM((2, SLOTS, SLOTS), f32),
            pltpu.VMEM((2,) + block, f32),
            pltpu.VMEM((2,) + block, f32),
            pltpu.VMEM((2,) + block, f32),
            pltpu.VMEM(block, f32),
            pltpu.VMEM((2,) + block, f32),
            pltpu.VMEM((2,) + block, f32),
            pltpu.VMEM((2,) + block, f32),
            pltpu.VMEM((8, 128), f32),
            pltpu.VMEM((plane, 8, 128), f32),
            pltpu.VMEM((8, 128), f32),
            pltpu.VMEM((ring, 8, 128), f32),
            dma((6,)),
            dma,
            dma((2,)),
            dma((2,)),
            dma((BLOCKS,)),
            dma((2, 2, BLOCKS)),
            dma((2, 2, BLOCKS)),
            dma((2, BLOCKS)),
            dma((2, BLOCKS)),
            dma((2, BLOCKS)),
            dma((2,)),
            dma((2,)),
        ],
        compiler_params=pltpu.CompilerParams(
            collective_id=0, has_side_effects=True, vmem_limit_bytes=40 << 20
        ),
        name="block_cg",
    )(right_side, coords, counts)


def solution(mesh):
    groups = mesh.shape["blk"]
    plane = 16 if groups % 16 == 0 else 2
    placed = (P(None, "blk"), P(None, "blk"), P("blk"), P(None, ("blk", "rep")))
    return jax.shard_map(
        functools.partial(on_device, groups, plane),
        mesh=mesh,
        in_specs=placed,
        out_specs=(P(None, "blk"), P(None, "blk")),
        check_vma=False,
    )
```

time: 1380 us -> 50.1 us (0.04)
  the two profiles are of different devices: /device:TPU:0 before, /device:TPU:5 now
where the time goes in v1:
time: 50.1 us; the launch traced here: 49.9 us
  Pallas kernels  45.7 us (91%)
  local copies, waits for them, and re-layouts  3.51 us (7%)
  between operations  0.65 us (1%)
    pallas_call x1, Pallas kernels, on_device(): pl.pallas_call(functools.partial(kernel, groups, plane), out_shape=(shape...  45.7 us
    unnamed x8, local copies, waits for them, and re-layouts  3.51 us

profile of v1, /device:TPU:5, one launch (start us, length us, event | category | flops | bytes accessed | tf_op | source)
XLA Modules:
  0.0 49.9 jit_solution(13461017654227336896)
XLA Ops:
  0.6 0.0 copy-start
  0.6 0.8 %copy-done = f32[8,2048]{1,0:T(8,128)S(1)} copy-done((f32[8,2048]{1,0:T(8,128)S(1)}, f32[8,2048]{1,0:T(8,128)}, u32[]{:S(2)}) %copy-start) | copy-done | bytes 65560
  1.5 0.0 copy-start.1
  1.5 0.8 %copy-done.1 = f32[3,2048]{1,0:T(4,128)S(1)} copy-done((f32[3,2048]{1,0:T(4,128)S(1)}, f32[3,2048]{1,0:T(4,128)}, u32[]{:S(2)}) %copy-start.1) | copy-done | bytes 24600
  2.2 0.0 copy-start.2
  2.2 0.7 %copy-done.2 = s32[4]{0:T(128)S(1)} copy-done((s32[4]{0:T(128)S(1)}, s32[4]{0:T(128)}, u32[]{:S(2)}) %copy-start.2) | copy-done | bytes 40
  2.9 45.7 %block_cg.1 = (f32[8,2048]{1,0:T(8,128)S(1)}, f32[8,2048]{1,0:T(8,128)S(1)}) custom-call(f32[8,2048]{1,0:T(8,128)S(1)} %copy-done, f32[3,2048]{1,0:T(4,128)S(1)} %copy-done.1, s32[4]{0:T(128)S(1)} %copy-done.2), custom_call_target="tpu_custom_call" | custom-call | tf_op jit(solution)/shard_map/block_cg/pallas_call | solution.py:501
  48.6 0.6 %copy.7 = f32[8,2048]{1,0:T(8,128)} copy(f32[8,2048]{1,0:T(8,128)S(1)} %get-tuple-element.4) | data formatting | bytes 131072
  49.2 0.6 %copy.8 = f32[8,2048]{1,0:T(8,128)} copy(f32[8,2048]{1,0:T(8,128)S(1)} %get-tuple-element.5) | data formatting | bytes 131072
Async XLA Ops:
  0.6 0.8 %copy-start = (f32[8,2048]{1,0:T(8,128)S(1)}, f32[8,2048]{1,0:T(8,128)}, u32[]{:S(2)}) copy-start(f32[8,2048]{1,0:T(8,128)} %rs_ref.1) | copy-start | bytes 196612
  1.5 0.8 %copy-start.1 = (f32[3,2048]{1,0:T(4,128)S(1)}, f32[3,2048]{1,0:T(4,128)}, u32[]{:S(2)}) copy-start(f32[3,2048]{1,0:T(4,128)} %co_ref.1) | copy-start | bytes 73732
  2.2 0.7 %copy-start.2 = (s32[4]{0:T(128)S(1)}, s32[4]{0:T(128)}, u32[]{:S(2)}) copy-start(s32[4]{0:T(128)} %cnt_ref.1) | copy-start | bytes 52

commit v2 on v1

v2 whole, which is shorter than its diff:
```python
import functools
import math

import jax
import jax.numpy as jnp
from jax import lax
from jax.experimental import pallas as pl
from jax.experimental.pallas import tpu as pltpu
from jax.sharding import PartitionSpec as P

SPAN = 4
BLOCKS = 4
SLOTS = 512
PROBES = 8
FAR = 5

sill = 0.1 / SPAN
nugget = 0.5
level = nugget + sill

KAPPA = math.sqrt(3.0) / (0.5 * SPAN) * math.log2(math.e)
REACH = SPAN * KAPPA
MATERN_ROOT = math.log2(math.e)
TAPER_ROOT = KAPPA * SPAN / 4.0
UNIT = REACH**4 * 2.0**REACH * MATERN_ROOT * TAPER_ROOT

ROWS = ((3, 0), (3, 0), (2, 0), (1, 1), (0, 1))
COLS = ((3, -1), (0, 1), (0, 2), (0, 1), (0, 1))
KEPT = ((1, 0), (0, 0), (0, 1), (0, 0), (0, 0))
ORDER = (0, 1, 5, 6, 7, 8, 9, 2, 3, 4)
CHUNK = 16
CHUNKS = SLOTS // CHUNK
XROW = 32

f32 = jnp.float32
bf16 = jnp.bfloat16
MESH = pl.DeviceIdType.MESH
HIGHEST = lax.Precision.HIGHEST
NT = (((1,), (1,)), ((), ()))


def split(x, parts):
    out = []
    for _ in range(parts - 1):
        piece = x.astype(bf16).astype(f32)
        out.append(piece)
        x = x - piece
    out.append(x.astype(bf16).astype(f32))
    return out


def two_parts(x):
    high = x.astype(bf16)
    low = (x - high.astype(f32)).astype(bf16)
    return jnp.concatenate([high, low], axis=0)


def mm(a, b):
    return jnp.dot(a, b, precision=HIGHEST, preferred_element_type=f32)


def inverse(matrix):
    rows = lax.broadcasted_iota(jnp.int32, (PROBES, PROBES), 0)
    eye = (rows == lax.broadcasted_iota(jnp.int32, (PROBES, PROBES), 1)).astype(f32)
    return eliminate(matrix, eye)


def eliminate(matrix, rhs):
    work = jnp.concatenate([matrix, rhs], axis=1)
    rows = lax.broadcasted_iota(jnp.int32, work.shape, 0)
    for k in range(PROBES):
        pivot = work[k : k + 1, k : k + 1]
        scaled = work[k : k + 1, :] / pivot
        column = jnp.broadcast_to(work[:, k : k + 1], work.shape)
        work = jnp.where(rows == k, scaled, work - column * scaled)
    return work[:, PROBES:]


def kernel(
    groups,
    plane,
    rs_ref,
    co_ref,
    cnt_ref,
    sol_ref,
    res_ref,
    cnt,
    co,
    geo_s,
    geo_r,
    qq,
    qn,
    alive,
    lraw,
    xc,
    lfeat,
    rraw,
    rfeat,
    xr,
    vrow,
    vnext,
    kc,
    yzs,
    tr,
    tc,
    other_in,
    spill_in,
    ahead_in,
    tile,
    sums,
    rhs,
    local_sem,
    geo_send,
    geo_recv,
    q_send,
    q_recv,
    mine_send,
    ahead_send,
    spill_send,
    other_recv,
    spill_recv,
    ahead_recv,
    red_send,
    red_recv,
):
    g = lax.axis_index("blk")
    c = lax.axis_index("rep")
    core = c.astype(f32)
    nxt = lax.rem(g + 1, groups)
    prv = lax.rem(g + groups - 1, groups)
    zs = groups // plane
    z, inplane = g // plane, lax.rem(g, plane)
    ring = zs * 2
    place = z * 2 + c

    def in_plane(k):
        return {"blk": z * plane + lax.rem(inplane + k, plane), "rep": c}

    def across(k):
        at = lax.rem(place + k, ring)
        return {"blk": (at // 2) * plane + inplane, "rep": lax.rem(at, 2)}

    def column(k):
        return c if k == 0 else 3 - c

    loads = [
        pltpu.make_async_copy(co_ref, co, local_sem.at[1]),
        pltpu.make_async_copy(cnt_ref, cnt, local_sem.at[0]),
    ]
    for b in range(BLOCKS):
        loads.append(
            pltpu.make_async_copy(
                rs_ref.at[:, pl.ds(b * SLOTS, SLOTS)], qq.at[b, 0:PROBES], local_sem.at[2 + b]
            )
        )
    for load in loads:
        load.start()

    barrier = pltpu.get_barrier_semaphore()

    def greet_plane(k, carry):
        pl.semaphore_signal(barrier, inc=1, device_id=in_plane(k), device_id_type=MESH)
        return carry

    def greet_across(k, carry):
        pl.semaphore_signal(barrier, inc=1, device_id=across(k), device_id_type=MESH)
        return carry

    for near in (prv, nxt):
        for side in (0, 1):
            pl.semaphore_signal(
                barrier, inc=1, device_id={"blk": near, "rep": side}, device_id_type=MESH
            )
    lax.fori_loop(1, ring, greet_across, 0)
    lax.fori_loop(1, plane, greet_plane, 0)

    for load in loads:
        load.wait()

    slot = lax.broadcasted_iota(jnp.int32, (1, SLOTS), 1)
    for b in range(BLOCKS):
        live = (slot < cnt[b]).astype(f32)
        alive[b] = live
        geo_s[b, 0:3] = co[:, b * SLOTS : (b + 1) * SLOTS]
        geo_s[b, 3:4] = live
        qq[b, 0:PROBES] = qq[b, 0:PROBES] * live

    pl.semaphore_wait(barrier, 4 + plane - 1 + ring - 1)

    def remote(src, dst, send_sem, recv_sem, blk, rep):
        return pltpu.make_async_remote_copy(
            src_ref=src,
            dst_ref=dst,
            send_sem=send_sem,
            recv_sem=recv_sem,
            device_id={"blk": blk, "rep": rep},
            device_id_type=MESH,
        )

    sends = []

    def send(*args):
        copy = remote(*args)
        copy.start()
        sends.append(copy)

    for k in range(2):
        at = column(k)
        send(geo_s.at[at, 0:4], geo_r.at[k, 0:4], geo_send.at[k], geo_recv.at[k], prv, c)
    for k in range(2):
        at = column(k)
        send(qq.at[at, 0:PROBES], qn.at[k, 0:PROBES], q_send.at[k], q_recv.at[k], prv, c)

    origin = geo_s[0, 0:1, 0:1]
    ones = jnp.ones((1, SLOTS), f32)

    def features(geo):
        x = (geo[0:1] - origin) * KAPPA
        y = (geo[1:2] - 0.5) * KAPPA
        w = (geo[2:3] - 0.5) * KAPPA
        return x, split(y, 3), split(w, 3), split(y * y + w * w, 3)

    def row_features(b):
        x, ys, ws, ns = features(geo_s[b])
        rows = []
        for q in (ys, ws):
            rows += [-2.0 * q[k] for k in (0, 0, 1, 1, 0, 2)]
        rows += ns + [ones] * 3
        for k, row in enumerate(rows):
            lraw[b, k : k + 1] = row
        lraw[b, XROW : XROW + 1] = x
        turned = lraw[b].T
        xc[b] = turned
        lfeat[b] = turned.astype(bf16)

    def column_features(geo, at):
        x, ys, ws, ns = features(geo)
        rows = []
        for q in (ys, ws):
            rows += [q[k] for k in (0, 1, 0, 1, 2, 0)]
        rows += [ones] * 3 + ns
        for k, row in enumerate(rows):
            rraw[at, k : k + 1] = row
        rfeat[at] = rraw[at].astype(bf16)
        xr[at] = x

    lraw[...] = jnp.zeros_like(lraw)
    rraw[...] = jnp.zeros_like(rraw)
    for k in range(2):
        column_features(geo_s[column(k)], k)
    for b in reversed(range(BLOCKS)):
        row_features(b)
        vrow[b] = two_parts(qq[b, 0:PROBES])

    def pick(table, n):
        low, step = table[n % 5]
        return low + step * c if step else low

    def kept(n):
        return pick(KEPT, n) + 2 * (n // 5)

    def build(n, chunk, half):
        s = pl.ds(chunk * CHUNK, CHUNK)
        along = xc[pick(ROWS, n), s, XROW : XROW + 1] - xr[kept(n)]
        square = jnp.maximum(along * along + yzs[half, s], 1e-12)
        dist = square * lax.rsqrt(square)
        inside = jnp.maximum(REACH - dist, 0.0)
        decay = jnp.exp2(inside)
        twice = inside * inside
        value = (twice * twice) * decay * ((dist + MATERN_ROOT) * (dist + TAPER_ROOT))
        high = value.astype(bf16)
        kc[n, s, 0:SLOTS] = high
        kc[n, s, SLOTS:] = (value - high.astype(f32)).astype(bf16)

    def across_part(n, quarter, half):
        s = pl.ds(quarter * 128, 128)
        yzs[half, s] = jnp.dot(
            lfeat[pick(ROWS, n), s], rfeat[kept(n)], preferred_element_type=f32
        )

    mirrored = {0: core, 2: 1.0 - core, 4: 0.0 * core}

    def apply(n, quarter, it):
        i = pick(ROWS, n)
        h = quarter % 2
        s = pl.ds(h * 256, 256)
        if quarter < 2:
            both = jnp.dot(
                vrow[i, :, h * 256 : h * 256 + 256], kc[n, s], preferred_element_type=f32
            )
            both = both[:, :SLOTS] + both[:, SLOTS:]
            part = both[:PROBES] + both[PROBES:]
            if n in mirrored:
                part = part * mirrored[n]
            if n < 5:
                tr[it, pick(COLS, n)] += part
            else:
                tc[it, pick(KEPT, n)] += part
        else:
            vec = vrow[pick(COLS, n)] if n < 5 else vnext[pick(KEPT, n)]
            both = lax.dot_general(vec, kc[n, s, 0:SLOTS], NT, preferred_element_type=f32)
            both += lax.dot_general(vec, kc[n, s, SLOTS:], NT, preferred_element_type=f32)
            tr[it, i, :, h * 256 : h * 256 + 256] += both[:PROBES] + both[PROBES:]

    tr[...] = jnp.zeros_like(tr)
    tc[...] = jnp.zeros_like(tc)

    def send_rows(b, it):
        send(tr.at[it, b], other_in.at[it, b], mine_send.at[it, b], other_recv.at[it, b], g, 1 - c)
        if it == 0:
            k, user = {0: (0, 0), 3: (1, 0), 1: (0, 1), 2: (1, 1)}[b]
            send(tr.at[it, b], ahead_in.at[c, k], ahead_send.at[b], ahead_recv.at[c, k], prv, user)

    def send_spill(k, it):
        at = column(k)
        for side in range(2):
            send(
                tc.at[it, k],
                spill_in.at[it, at],
                spill_send.at[side, it, k],
                spill_recv.at[it, at],
                nxt,
                side,
            )

    def wait_for(dst, sem):
        pltpu.make_async_copy(dst, dst, sem).wait()

    def gather_block(b, it):
        wait_for(other_in.at[it, b], other_recv.at[it, b])
        wait_for(spill_in.at[it, b], spill_recv.at[it, b])
        total = (tr[it, b] + other_in[it, b]) + spill_in[it, b]
        old = qq[b, it * PROBES : (it + 1) * PROBES]
        qq[b, (it + 1) * PROBES : (it + 2) * PROBES] = total * (alive[b] * (1.0 / UNIT)) - old

    def gather_ahead(k):
        for side in range(2):
            wait_for(ahead_in.at[side, k], ahead_recv.at[side, k])
        total = (ahead_in[0, k] + ahead_in[1, k]) + tc[0, k]
        qn[k, PROBES:] = total * (geo_r[k, 3:4] * (1.0 / UNIT)) - qn[k, 0:PROBES]

    for quarter in range(4):
        across_part(ORDER[0], quarter, 0)
    for at, n in enumerate(ORDER):
        then = ORDER[at + 1] if at + 1 < len(ORDER) else None
        if at == 1:
            for k in range(2):
                wait_for(geo_r.at[k, 0:4], geo_recv.at[k])
                column_features(geo_r[k], 2 + k)
        if at == 2:
            for k in range(2):
                wait_for(qn.at[k, 0:PROBES], q_recv.at[k])
                vnext[k] = two_parts(qn[k, 0:PROBES])
        for chunk in range(CHUNKS):
            build(n, chunk, at % 2)
            if chunk % 8 == 3 and then is not None:
                across_part(then, chunk // 8, (at + 1) % 2)
            if chunk % 8 == 7 and at > 0:
                apply(ORDER[at - 1], chunk // 8, 0)
        if at == 4:
            send_rows(3, 0)
        if at == 5:
            send_spill(1, 0)
        if at == 7:
            send_spill(0, 0)
        if at == 9:
            send_rows(2, 0)
    for quarter in range(4):
        apply(ORDER[-1], quarter, 0)
    send_rows(1, 0)
    send_rows(0, 0)

    def ready(b):
        gather_block(b, 0)
        vrow[b] = two_parts(qq[b, PROBES : 2 * PROBES])

    def second(n):
        for quarter in range(4):
            apply(n, quarter, 1)

    ready(3)
    ready(2)
    second(0)
    ready(1)
    ready(0)
    for n in range(1, 5):
        second(n)

    def spread(turn, count, target):
        me = inplane if turn % 2 == 0 else place
        src, dst = tile.at[turn], sums.at[turn]

        def one(step, carry):
            pltpu.make_async_remote_copy(
                src_ref=src,
                dst_ref=dst.at[me],
                send_sem=red_send.at[turn],
                recv_sem=red_recv.at[turn],
                device_id=target(step),
                device_id_type=MESH,
            ).start()
            return carry

        lax.fori_loop(1, count, one, 0)
        dst[me] = src[...]

    def total_of(turn, count):
        everything = sums.at[turn, pl.ds(0, count - 1)]
        pltpu.make_async_copy(everything, everything, red_recv.at[turn]).wait()
        parts = [sums[turn, at] for at in range(count)]
        while len(parts) > 1:
            parts = [sum(parts[at : at + 2]) for at in range(0, len(parts), 2)]
        return parts[0]

    tile[...] = jnp.zeros_like(tile)
    gram = jnp.zeros((2 * PROBES, 2 * PROBES), f32)
    for b in range(2):
        pair = qq[2 * c + b, 0 : 2 * PROBES]
        gram += lax.dot_general(pair, pair, NT, precision=HIGHEST, preferred_element_type=f32)
    tile[0, :, 0:16] = gram[0:PROBES]
    tile[0, :, 16:32] = gram[PROBES:]
    spread(0, plane, in_plane)

    for k in range(2):
        gather_ahead(k)
        vnext[k] = two_parts(qn[k, PROBES:])
    for n in range(5, 10):
        second(n)

    part = jnp.zeros((PROBES, PROBES), f32)
    for b in range(BLOCKS):
        part += lax.dot_general(
            qq[b, PROBES : 2 * PROBES], tr[1, b], NT, precision=HIGHEST, preferred_element_type=f32
        )
    for k in range(2):
        part += lax.dot_general(
            qn[k, PROBES:], tc[1, k], NT, precision=HIGHEST, preferred_element_type=f32
        )
    tile[2, :, 0:8] = part * (1.0 / UNIT)
    spread(2, plane, in_plane)
    for k in range(2):
        send_spill(k, 1)
    for b in range(BLOCKS):
        send_rows(b, 1)

    tile[1] = total_of(0, plane)
    spread(1, ring, across)
    tile[3] = total_of(2, plane)
    spread(3, ring, across)
    early = total_of(1, ring)

    h00, h01, h11 = early[:, 0:8], early[:, 8:16], early[:, 24:32]
    curv_inv = inverse(level * h00 + sill * h01)
    alpha = mm(curv_inv, h00)
    m2 = mm(curv_inv, h01)
    m1 = mm(curv_inv, h11)
    alpha_t = mm(h00, curv_inv)
    w_t = sill * mm(h01, curv_inv)
    n_fwd = sill * (mm(h00, m1) - mm(h01, m2))
    n_t = sill * (mm(h11, alpha) - mm(h01, m2))
    beta = sill * mm(curv_inv, n_t)
    beta_t = sill * mm(n_fwd, curv_inv)
    new = mm(h00, beta)
    f_fwd = sill * m2 + beta
    f_t = w_t + beta_t
    known = level * new - sill * mm(n_fwd, f_fwd) - sill**3 * mm(mm(h01, m1), alpha)
    known -= sill**3 * mm(mm(alpha_t, h11), alpha)
    right = jnp.concatenate([f_t, sill * alpha_t], axis=1)
    zero = jnp.zeros((PROBES, PROBES), f32)
    first = jnp.concatenate(
        [
            jnp.concatenate([alpha_t, zero], axis=1),
            jnp.concatenate([w_t, -sill * alpha_t], axis=1),
        ],
        axis=0,
    )
    for b in range(BLOCKS):
        s = pl.ds(b * SLOTS, SLOTS)
        start = mm(first, qq[b, 0 : 2 * PROBES])
        sol_ref[:, s] = start[:PROBES]
        res_ref[:, s] = start[PROBES:]
        gather_block(b, 1)
        q0, q1, q2 = (qq[b, k * PROBES : (k + 1) * PROBES] for k in range(3))
        rhs[b, 0:PROBES, 0:SLOTS] = q0
        rhs[b, PROBES:, 0:SLOTS] = -q1
        rhs[b, 0:PROBES, SLOTS:] = -(level * q0 + sill * q1)
        rhs[b, PROBES:, SLOTS:] = level * q1 + sill * q2

    late = total_of(3, ring)
    curv = known + sill**3 * mm(mm(alpha_t, late[:, 0:8]), alpha)
    weights = mm(new, eliminate(curv, right))
    for b in range(BLOCKS):
        s = pl.ds(b * SLOTS, SLOTS)
        more = mm(weights, rhs[b])
        sol_ref[:, s] += more[:, :SLOTS]
        res_ref[:, s] += more[:, SLOTS:]

    for copy in sends:
        copy.wait_send()
    for turn in range(4):
        everything = sums.at[turn, pl.ds(0, (plane if turn % 2 == 0 else ring) - 1)]
        pltpu.make_async_copy(everything, everything, red_send.at[turn]).wait()


def on_device(groups, plane, right_side, coords, counts, pair_list):
    del pair_list
    ring = groups // plane * 2
    block = (BLOCKS, PROBES, SLOTS)
    dma = pltpu.SemaphoreType.DMA
    width = right_side.shape[1]
    shape = jax.ShapeDtypeStruct((PROBES, width), f32)
    anywhere = pl.BlockSpec(memory_space=pl.ANY)
    vmem = pl.BlockSpec(memory_space=pltpu.VMEM)
    return pl.pallas_call(
        functools.partial(kernel, groups, plane),
        out_shape=(shape, shape),
        in_specs=[anywhere] * 3,
        out_specs=(vmem, vmem),
        scratch_shapes=[
            pltpu.SMEM((BLOCKS,), jnp.int32),
            pltpu.VMEM((3, width), f32),
            pltpu.VMEM(block, f32),
            pltpu.VMEM((2, PROBES, SLOTS), f32),
            pltpu.VMEM((BLOCKS, 3 * PROBES, SLOTS), f32),
            pltpu.VMEM((2, 2 * PROBES, SLOTS), f32),
            pltpu.VMEM((BLOCKS, 1, SLOTS), f32),
            pltpu.VMEM((BLOCKS, 128, SLOTS), f32),
            pltpu.VMEM((BLOCKS, SLOTS, 128), f32),
            pltpu.VMEM((BLOCKS, SLOTS, 128), bf16),
            pltpu.VMEM((BLOCKS, 128, SLOTS), f32),
            pltpu.VMEM((BLOCKS, 128, SLOTS), bf16),
            pltpu.VMEM((BLOCKS, 1, SLOTS), f32),
            pltpu.VMEM((BLOCKS, 2 * PROBES, SLOTS), bf16),
            pltpu.VMEM((2, 2 * PROBES, SLOTS), bf16),
            pltpu.VMEM((len(ORDER), SLOTS, 2 * SLOTS), bf16),
            pltpu.VMEM((2, SLOTS, SLOTS), f32),
            pltpu.VMEM((2,) + block, f32),
            pltpu.VMEM((2, 2, PROBES, SLOTS), f32),
            pltpu.VMEM((2,) + block, f32),
            pltpu.VMEM((2,) + block, f32),
            pltpu.VMEM((2, 2, PROBES, SLOTS), f32),
            pltpu.VMEM((4, 8, 128), f32),
            pltpu.VMEM((4, max(plane, ring), 8, 128), f32),
            pltpu.VMEM((BLOCKS, 2 * PROBES, 2 * SLOTS), f32),
            dma((6,)),
            dma((2,)),
            dma((2,)),
            dma((2,)),
            dma((2,)),
            dma((2, BLOCKS)),
            dma((BLOCKS,)),
            dma((2, 2, 2)),
            dma((2, BLOCKS)),
            dma((2, BLOCKS)),
            dma((2, 2)),
            dma((4,)),
            dma((4,)),
        ],
        compiler_params=pltpu.CompilerParams(
            collective_id=0, has_side_effects=True, vmem_limit_bytes=60 << 20
        ),
        name="block_cg",
    )(right_side, coords, counts)


def solution(mesh):
    groups = mesh.shape["blk"]
    plane = 16 if groups % 16 == 0 else 2
    placed = (P(None, "blk"), P(None, "blk"), P("blk"), P(None, ("blk", "rep")))
    return jax.shard_map(
        functools.partial(on_device, groups, plane),
        mesh=mesh,
        in_specs=placed,
        out_specs=(P(None, "blk"), P(None, "blk")),
        check_vma=False,
    )
```

time: 50.1 us -> 47.9 us (0.956)
  the two profiles are of different devices: /device:TPU:5 before, /device:TPU:1 now
where the time goes in v2:
time: 47.9 us; the launch traced here: 47.7 us
  Pallas kernels  45 us (94%)
  local copies, waits for them, and re-layouts  2.14 us (4%)
  between operations  0.65 us (1%)
    pallas_call x1, Pallas kernels, on_device(): pl.pallas_call(functools.partial(kernel, groups, plane), out_shape=(shape...  45 us
    unnamed x4, local copies, waits for them, and re-layouts  2.14 us

profile of v2, /device:TPU:1, one launch (start us, length us, event | category | flops | bytes accessed | tf_op | source)
XLA Modules:
  0.0 47.7 jit_solution(14074195859204261752)
XLA Ops:
  0.6 45.0 %block_cg.1 = (f32[8,2048]{1,0:T(8,128)}, f32[8,2048]{1,0:T(8,128)}) custom-call(f32[8,2048]{1,0:T(8,128)} %rs_ref.1, f32[3,2048]{1,0:T(4,128)} %co_ref.1, s32[4]{0:T(128)} %cnt_ref.1), custom_call_target="tpu_custom_call" | custom-call | tf_op jit(solution)/shard_map/block_cg/pallas_call | solution.py:514
  45.6 0.0 copy-start
  45.6 1.5 %copy.7 = f32[8,2048]{1,0:T(8,128)} copy(f32[8,2048]{1,0:T(8,128)} %get-tuple-element.4) | data formatting | bytes 131072
  47.1 0.0 copy-done
  47.1 0.6 %copy.8 = f32[8,2048]{1,0:T(8,128)} copy(f32[8,2048]{1,0:T(8,128)S(1)} %copy-done) | data formatting | bytes 131072
Async XLA Ops:
  45.6 1.5 %copy-start = (f32[8,2048]{1,0:T(8,128)S(1)}, f32[8,2048]{1,0:T(8,128)}, u32[]{:S(2)}) copy-start(f32[8,2048]{1,0:T(8,128)} %get-tuple-element.5) | copy-start | bytes 196612

commit v3 on v2

--- a/solution.py
+++ b/solution.py
@@ -18,15 +18,16 @@
 nugget = 0.5
 level = nugget + sill
 
-KAPPA = math.sqrt(3.0) / (0.5 * SPAN) * math.log2(math.e)
+KAPPA = math.sqrt(3.0) / (0.5 * SPAN)
 REACH = SPAN * KAPPA
-MATERN_ROOT = math.log2(math.e)
+MATERN_ROOT = 1.0
 TAPER_ROOT = KAPPA * SPAN / 4.0
-UNIT = REACH**4 * 2.0**REACH * MATERN_ROOT * TAPER_ROOT
-
-ROWS = ((3, 0), (3, 0), (2, 0), (1, 1), (0, 1))
-COLS = ((3, -1), (0, 1), (0, 2), (0, 1), (0, 1))
-KEPT = ((1, 0), (0, 0), (0, 1), (0, 0), (0, 0))
+UNIT = REACH**4 * math.exp(REACH) * MATERN_ROOT * TAPER_ROOT
+
+ROWS = ((3, -1), (3, 0), (2, 1), (1, 1), (0, 1))
+COLS = ((3, -1), (0, 2), (0, 1), (0, 1), (0, 1))
+KEPT = ((1, 0), (0, 1), (0, 0), (0, 0), (0, 0))
+DIAGONAL = (0, 4)
 ORDER = (0, 1, 5, 6, 7, 8, 9, 2, 3, 4)
 CHUNK = 16
 CHUNKS = SLOTS // CHUNK
@@ -56,7 +57,10 @@
 
 
 def mm(a, b):
-    return jnp.dot(a, b, precision=HIGHEST, preferred_element_type=f32)
+    terms = [a[:, k : k + 1] * b[k : k + 1] for k in range(PROBES)]
+    while len(terms) > 1:
+        terms = [functools.reduce(jnp.add, terms[at : at + 2]) for at in range(0, len(terms), 2)]
+    return terms[0]
 
 
 def inverse(matrix):
@@ -82,8 +86,7 @@
     rs_ref,
     co_ref,
     cnt_ref,
-    sol_ref,
-    res_ref,
+    out_ref,
     cnt,
     co,
     geo_s,
@@ -125,7 +128,6 @@
 ):
     g = lax.axis_index("blk")
     c = lax.axis_index("rep")
-    core = c.astype(f32)
     nxt = lax.rem(g + 1, groups)
     prv = lax.rem(g + groups - 1, groups)
     zs = groups // plane
@@ -265,7 +267,7 @@
         square = jnp.maximum(along * along + yzs[half, s], 1e-12)
         dist = square * lax.rsqrt(square)
         inside = jnp.maximum(REACH - dist, 0.0)
-        decay = jnp.exp2(inside)
+        decay = jnp.exp(inside)
         twice = inside * inside
         value = (twice * twice) * decay * ((dist + MATERN_ROOT) * (dist + TAPER_ROOT))
         high = value.astype(bf16)
@@ -278,20 +280,18 @@
             lfeat[pick(ROWS, n), s], rfeat[kept(n)], preferred_element_type=f32
         )
 
-    mirrored = {0: core, 2: 1.0 - core, 4: 0.0 * core}
-
     def apply(n, quarter, it):
         i = pick(ROWS, n)
         h = quarter % 2
         s = pl.ds(h * 256, 256)
+        if quarter < 2 and n in DIAGONAL:
+            return
         if quarter < 2:
             both = jnp.dot(
                 vrow[i, :, h * 256 : h * 256 + 256], kc[n, s], preferred_element_type=f32
             )
             both = both[:, :SLOTS] + both[:, SLOTS:]
             part = both[:PROBES] + both[PROBES:]
-            if n in mirrored:
-                part = part * mirrored[n]
             if n < 5:
                 tr[it, pick(COLS, n)] += part
             else:
@@ -343,26 +343,29 @@
         across_part(ORDER[0], quarter, 0)
     for at, n in enumerate(ORDER):
         then = ORDER[at + 1] if at + 1 < len(ORDER) else None
-        if at == 1:
-            for k in range(2):
-                wait_for(geo_r.at[k, 0:4], geo_recv.at[k])
-                column_features(geo_r[k], 2 + k)
         if at == 2:
             for k in range(2):
                 wait_for(qn.at[k, 0:PROBES], q_recv.at[k])
                 vnext[k] = two_parts(qn[k, 0:PROBES])
         for chunk in range(CHUNKS):
+            if at == 1 and chunk == CHUNKS // 2:
+                for k in range(2):
+                    wait_for(geo_r.at[k, 0:4], geo_recv.at[k])
+                    column_features(geo_r[k], 2 + k)
             build(n, chunk, at % 2)
-            if chunk % 8 == 3 and then is not None:
+            if at == 1:
+                if chunk >= CHUNKS // 2 and chunk % 4 == 1:
+                    across_part(then, (chunk - CHUNKS // 2) // 4, (at + 1) % 2)
+            elif chunk % 8 == 3 and then is not None:
                 across_part(then, chunk // 8, (at + 1) % 2)
             if chunk % 8 == 7 and at > 0:
                 apply(ORDER[at - 1], chunk // 8, 0)
         if at == 4:
-            send_rows(3, 0)
-        if at == 5:
             send_spill(1, 0)
         if at == 7:
             send_spill(0, 0)
+        if at == 8:
+            send_rows(3, 0)
         if at == 9:
             send_rows(2, 0)
     for quarter in range(4):
@@ -370,24 +373,7 @@
     send_rows(1, 0)
     send_rows(0, 0)
 
-    def ready(b):
-        gather_block(b, 0)
-        vrow[b] = two_parts(qq[b, PROBES : 2 * PROBES])
-
-    def second(n):
-        for quarter in range(4):
-            apply(n, quarter, 1)
-
-    ready(3)
-    ready(2)
-    second(0)
-    ready(1)
-    ready(0)
-    for n in range(1, 5):
-        second(n)
-
-    def spread(turn, count, target):
-        me = inplane if turn % 2 == 0 else place
+    def spread(turn, me, count, target):
         src, dst = tile.at[turn], sums.at[turn]
 
         def one(step, carry):
@@ -409,8 +395,25 @@
         pltpu.make_async_copy(everything, everything, red_recv.at[turn]).wait()
         parts = [sums[turn, at] for at in range(count)]
         while len(parts) > 1:
-            parts = [sum(parts[at : at + 2]) for at in range(0, len(parts), 2)]
+            parts = [functools.reduce(jnp.add, parts[at : at + 2]) for at in range(0, len(parts), 2)]
         return parts[0]
+
+    def ready(b):
+        gather_block(b, 0)
+        vrow[b] = two_parts(qq[b, PROBES : 2 * PROBES])
+
+    def second(n):
+        for quarter in range(4):
+            apply(n, quarter, 1)
+
+    ready(3)
+    ready(2)
+    second(0)
+    ready(1)
+    ready(0)
+
+    for n in range(1, 5):
+        second(n)
 
     tile[...] = jnp.zeros_like(tile)
     gram = jnp.zeros((2 * PROBES, 2 * PROBES), f32)
@@ -419,7 +422,6 @@
         gram += lax.dot_general(pair, pair, NT, precision=HIGHEST, preferred_element_type=f32)
     tile[0, :, 0:16] = gram[0:PROBES]
     tile[0, :, 16:32] = gram[PROBES:]
-    spread(0, plane, in_plane)
 
     for k in range(2):
         gather_ahead(k)
@@ -436,69 +438,51 @@
         part += lax.dot_general(
             qn[k, PROBES:], tc[1, k], NT, precision=HIGHEST, preferred_element_type=f32
         )
-    tile[2, :, 0:8] = part * (1.0 / UNIT)
-    spread(2, plane, in_plane)
+    tile[0, :, 32:40] = part * (1.0 / UNIT)
+    spread(0, inplane, plane, in_plane)
     for k in range(2):
         send_spill(k, 1)
     for b in range(BLOCKS):
         send_rows(b, 1)
-
     tile[1] = total_of(0, plane)
-    spread(1, ring, across)
-    tile[3] = total_of(2, plane)
-    spread(3, ring, across)
-    early = total_of(1, ring)
-
-    h00, h01, h11 = early[:, 0:8], early[:, 8:16], early[:, 24:32]
+    spread(1, place, ring, across)
+
+    for b in range(BLOCKS):
+        gather_block(b, 1)
+        for k in range(3 * PROBES):
+            rhs[b, k] = jnp.broadcast_to(qq[b, k : k + 1], (PROBES, SLOTS))
+
+    totals = total_of(1, ring)
+    h00, h01, h11 = totals[:, 0:8], totals[:, 8:16], totals[:, 24:32]
     curv_inv = inverse(level * h00 + sill * h01)
-    alpha = mm(curv_inv, h00)
-    m2 = mm(curv_inv, h01)
-    m1 = mm(curv_inv, h11)
+    left = mm(curv_inv, totals[:, 0:40])
+    alpha, m2, m1, m12 = (left[:, at : at + PROBES] for at in (0, 8, 24, 32))
     alpha_t = mm(h00, curv_inv)
     w_t = sill * mm(h01, curv_inv)
-    n_fwd = sill * (mm(h00, m1) - mm(h01, m2))
-    n_t = sill * (mm(h11, alpha) - mm(h01, m2))
+    middle = mm(h01, m2)
+    n_fwd = sill * (mm(h00, m1) - middle)
+    n_t = sill * (mm(h11, alpha) - middle)
     beta = sill * mm(curv_inv, n_t)
     beta_t = sill * mm(n_fwd, curv_inv)
     new = mm(h00, beta)
-    f_fwd = sill * m2 + beta
-    f_t = w_t + beta_t
-    known = level * new - sill * mm(n_fwd, f_fwd) - sill**3 * mm(mm(h01, m1), alpha)
-    known -= sill**3 * mm(mm(alpha_t, h11), alpha)
-    right = jnp.concatenate([f_t, sill * alpha_t], axis=1)
-    zero = jnp.zeros((PROBES, PROBES), f32)
-    first = jnp.concatenate(
-        [
-            jnp.concatenate([alpha_t, zero], axis=1),
-            jnp.concatenate([w_t, -sill * alpha_t], axis=1),
-        ],
-        axis=0,
-    )
-    for b in range(BLOCKS):
-        s = pl.ds(b * SLOTS, SLOTS)
-        start = mm(first, qq[b, 0 : 2 * PROBES])
-        sol_ref[:, s] = start[:PROBES]
-        res_ref[:, s] = start[PROBES:]
-        gather_block(b, 1)
-        q0, q1, q2 = (qq[b, k * PROBES : (k + 1) * PROBES] for k in range(3))
-        rhs[b, 0:PROBES, 0:SLOTS] = q0
-        rhs[b, PROBES:, 0:SLOTS] = -q1
-        rhs[b, 0:PROBES, SLOTS:] = -(level * q0 + sill * q1)
-        rhs[b, PROBES:, SLOTS:] = level * q1 + sill * q2
-
-    late = total_of(3, ring)
-    curv = known + sill**3 * mm(mm(alpha_t, late[:, 0:8]), alpha)
-    weights = mm(new, eliminate(curv, right))
-    for b in range(BLOCKS):
-        s = pl.ds(b * SLOTS, SLOTS)
-        more = mm(weights, rhs[b])
-        sol_ref[:, s] += more[:, :SLOTS]
-        res_ref[:, s] += more[:, SLOTS:]
+    inner = mm(h00, m12 - m1) - mm(h01, m1)
+    curv = level * new - sill * mm(n_fwd, sill * m2 + beta) + sill**3 * mm(inner, alpha)
+    x_y = mm(new, eliminate(curv, jnp.concatenate([w_t + beta_t, sill * alpha_t], axis=1)))
+    x_t, y_t = x_y[:, :PROBES], x_y[:, PROBES:]
+    top = (alpha_t + x_t, -y_t)
+    low = (w_t - level * x_t, level * y_t - sill * x_t - sill * alpha_t, sill * y_t)
+    for h, weights in enumerate((top, low)):
+        columns = [part[:, k : k + 1] for part in weights for k in range(PROBES)]
+        for b in range(BLOCKS):
+            terms = [column * rhs[b, k] for k, column in enumerate(columns)]
+            while len(terms) > 1:
+                terms = [functools.reduce(jnp.add, terms[at : at + 2]) for at in range(0, len(terms), 2)]
+            out_ref[h * PROBES : (h + 1) * PROBES, b * SLOTS : (b + 1) * SLOTS] = terms[0]
 
     for copy in sends:
         copy.wait_send()
-    for turn in range(4):
-        everything = sums.at[turn, pl.ds(0, (plane if turn % 2 == 0 else ring) - 1)]
+    for turn, count in enumerate((plane, ring)):
+        everything = sums.at[turn, pl.ds(0, count - 1)]
         pltpu.make_async_copy(everything, everything, red_send.at[turn]).wait()
 
 
@@ -508,14 +492,14 @@
     block = (BLOCKS, PROBES, SLOTS)
     dma = pltpu.SemaphoreType.DMA
     width = right_side.shape[1]
-    shape = jax.ShapeDtypeStruct((PROBES, width), f32)
+    shape = jax.ShapeDtypeStruct((2 * PROBES, width), f32)
     anywhere = pl.BlockSpec(memory_space=pl.ANY)
     vmem = pl.BlockSpec(memory_space=pltpu.VMEM)
-    return pl.pallas_call(
+    both = pl.pallas_call(
         functools.partial(kernel, groups, plane),
-        out_shape=(shape, shape),
+        out_shape=shape,
         in_specs=[anywhere] * 3,
-        out_specs=(vmem, vmem),
+        out_specs=vmem,
         scratch_shapes=[
             pltpu.SMEM((BLOCKS,), jnp.int32),
             pltpu.VMEM((3, width), f32),
@@ -539,9 +523,9 @@
             pltpu.VMEM((2,) + block, f32),
             pltpu.VMEM((2,) + block, f32),
             pltpu.VMEM((2, 2, PROBES, SLOTS), f32),
-            pltpu.VMEM((4, 8, 128), f32),
-            pltpu.VMEM((4, max(plane, ring), 8, 128), f32),
-            pltpu.VMEM((BLOCKS, 2 * PROBES, 2 * SLOTS), f32),
+            pltpu.VMEM((2, 8, 128), f32),
+            pltpu.VMEM((2, max(plane, ring), 8, 128), f32),
+            pltpu.VMEM((BLOCKS, 3 * PROBES, PROBES, SLOTS), f32),
             dma((6,)),
             dma((2,)),
             dma((2,)),
@@ -553,14 +537,15 @@
             dma((2, BLOCKS)),
             dma((2, BLOCKS)),
             dma((2, 2)),
-            dma((4,)),
-            dma((4,)),
+            dma((2,)),
+            dma((2,)),
         ],
         compiler_params=pltpu.CompilerParams(
             collective_id=0, has_side_effects=True, vmem_limit_bytes=60 << 20
         ),
         name="block_cg",
     )(right_side, coords, counts)
+    return both[:PROBES], both[PROBES:]
 
 
 def solution(mesh):

time: 47.9 us -> 45.6 us (0.952)
  Pallas kernels: 45 us -> 43.2 us
  local copies, waits for them, and re-layouts: 2.14 us -> 1.53 us
    unnamed x4 -> x0, local copies, waits for them, and re-layouts: 2.14 us -> none
    pallas_call x1, Pallas kernels: 45 us -> 43.2 us  [on_device(): pl.pallas_call(functools.partial(kernel, groups, plane), out_shape=shape,...]
    slice x0 -> x1, local copies, waits for them, and re-layouts: none -> 1.53 us  [on_device(): return (both[:PROBES], both[PROBES:])]
where the time goes in v3:
time: 45.6 us; the launch traced here: 45.4 us
  Pallas kernels  43.2 us (95%)
  local copies, waits for them, and re-layouts  1.53 us (3%)
  between operations  0.64 us (1%)
    pallas_call x1, Pallas kernels, on_device(): pl.pallas_call(functools.partial(kernel, groups, plane), out_shape=shape,...  43.2 us
    slice x1, local copies, waits for them, and re-layouts, on_device(): return (both[:PROBES], both[PROBES:])  1.53 us

profile of v3, /device:TPU:1, one launch (start us, length us, event | category | flops | bytes accessed | tf_op | source)
XLA Modules:
  0.0 45.4 jit_solution(1359377910092532277)
XLA Ops:
  0.6 43.2 %block_cg.1 = f32[16,2048]{1,0:T(8,128)} custom-call(f32[8,2048]{1,0:T(8,128)} %rs_ref.1, f32[3,2048]{1,0:T(4,128)} %co_ref.1, s32[4]{0:T(128)} %cnt_ref.1), custom_call_target="tpu_custom_call" | custom-call | tf_op jit(solution)/shard_map/block_cg/pallas_call | solution.py:498
  43.9 1.5 %fusion = (f32[8,2048]{1,0:T(8,128)}, f32[8,2048]{1,0:T(8,128)}) fusion(f32[16,2048]{1,0:T(8,128)} %block_cg.1), kind=kLoop, calls=%fused_computation | loop fusion | bytes 262144 | tf_op jit(solution)/shard_map/slice | solution.py:548

commit v4 on v3

--- a/solution.py
+++ b/solution.py
@@ -28,6 +28,7 @@
 COLS = ((3, -1), (0, 2), (0, 1), (0, 1), (0, 1))
 KEPT = ((1, 0), (0, 1), (0, 0), (0, 0), (0, 0))
 DIAGONAL = (0, 4)
+SPILLED = ((0, 0), (1, 0), (1, 1), (0, 1))
 ORDER = (0, 1, 5, 6, 7, 8, 9, 2, 3, 4)
 CHUNK = 16
 CHUNKS = SLOTS // CHUNK
@@ -36,7 +37,6 @@
 f32 = jnp.float32
 bf16 = jnp.bfloat16
 MESH = pl.DeviceIdType.MESH
-HIGHEST = lax.Precision.HIGHEST
 NT = (((1,), (1,)), ((), ()))
 
 
@@ -90,7 +90,9 @@
     cnt,
     co,
     geo_s,
+    geo_out,
     geo_r,
+    q_out,
     qq,
     qn,
     alive,
@@ -138,6 +140,9 @@
     def in_plane(k):
         return {"blk": z * plane + lax.rem(inplane + k, plane), "rep": c}
 
+    def along_z(k):
+        return {"blk": lax.rem(z + k, zs) * plane + inplane, "rep": c}
+
     def across(k):
         at = lax.rem(place + k, ring)
         return {"blk": (at // 2) * plane + inplane, "rep": lax.rem(at, 2)}
@@ -207,11 +212,10 @@
         sends.append(copy)
 
     for k in range(2):
-        at = column(k)
-        send(geo_s.at[at, 0:4], geo_r.at[k, 0:4], geo_send.at[k], geo_recv.at[k], prv, c)
-    for k in range(2):
-        at = column(k)
-        send(qq.at[at, 0:PROBES], qn.at[k, 0:PROBES], q_send.at[k], q_recv.at[k], prv, c)
+        geo_out[4 * k : 4 * k + 4] = geo_s[column(k), 0:4]
+        q_out[k] = qq[column(k), 0:PROBES]
+    send(geo_out, geo_r, geo_send, geo_recv, prv, c)
+    send(q_out, qn.at[0], q_send, q_recv, prv, c)
 
     origin = geo_s[0, 0:1, 0:1]
     ones = jnp.ones((1, SLOTS), f32)
@@ -305,20 +309,27 @@
     tr[...] = jnp.zeros_like(tr)
     tc[...] = jnp.zeros_like(tc)
 
-    def send_rows(b, it):
-        send(tr.at[it, b], other_in.at[it, b], mine_send.at[it, b], other_recv.at[it, b], g, 1 - c)
-        if it == 0:
-            k, user = {0: (0, 0), 3: (1, 0), 1: (0, 1), 2: (1, 1)}[b]
-            send(tr.at[it, b], ahead_in.at[c, k], ahead_send.at[b], ahead_recv.at[c, k], prv, user)
+    def send_rows(low, high, it):
+        send(
+            tr.at[it, low:high],
+            other_in.at[it, low:high],
+            mine_send.at[it, low],
+            other_recv.at[it, low],
+            g,
+            1 - c,
+        )
+
+    def send_ahead(b):
+        k, user = {0: (0, 0), 3: (1, 0), 1: (0, 1), 2: (1, 1)}[b]
+        send(tr.at[0, b], ahead_in.at[c, k], ahead_send.at[b], ahead_recv.at[c, k], prv, user)
 
     def send_spill(k, it):
-        at = column(k)
         for side in range(2):
             send(
                 tc.at[it, k],
-                spill_in.at[it, at],
+                spill_in.at[it, c, k],
                 spill_send.at[side, it, k],
-                spill_recv.at[it, at],
+                spill_recv.at[it, c, k],
                 nxt,
                 side,
             )
@@ -327,9 +338,9 @@
         pltpu.make_async_copy(dst, dst, sem).wait()
 
     def gather_block(b, it):
-        wait_for(other_in.at[it, b], other_recv.at[it, b])
-        wait_for(spill_in.at[it, b], spill_recv.at[it, b])
-        total = (tr[it, b] + other_in[it, b]) + spill_in[it, b]
+        side, k = SPILLED[b]
+        wait_for(spill_in.at[it, side, k], spill_recv.at[it, side, k])
+        total = (tr[it, b] + other_in[it, b]) + spill_in[it, side, k]
         old = qq[b, it * PROBES : (it + 1) * PROBES]
         qq[b, (it + 1) * PROBES : (it + 2) * PROBES] = total * (alive[b] * (1.0 / UNIT)) - old
 
@@ -337,21 +348,21 @@
         for side in range(2):
             wait_for(ahead_in.at[side, k], ahead_recv.at[side, k])
         total = (ahead_in[0, k] + ahead_in[1, k]) + tc[0, k]
-        qn[k, PROBES:] = total * (geo_r[k, 3:4] * (1.0 / UNIT)) - qn[k, 0:PROBES]
+        qn[1, k] = total * (geo_r[4 * k + 3 : 4 * k + 4] * (1.0 / UNIT)) - qn[0, k]
 
     for quarter in range(4):
         across_part(ORDER[0], quarter, 0)
     for at, n in enumerate(ORDER):
         then = ORDER[at + 1] if at + 1 < len(ORDER) else None
         if at == 2:
+            wait_for(qn.at[0], q_recv)
             for k in range(2):
-                wait_for(qn.at[k, 0:PROBES], q_recv.at[k])
-                vnext[k] = two_parts(qn[k, 0:PROBES])
+                vnext[k] = two_parts(qn[0, k])
         for chunk in range(CHUNKS):
             if at == 1 and chunk == CHUNKS // 2:
+                wait_for(geo_r, geo_recv)
                 for k in range(2):
-                    wait_for(geo_r.at[k, 0:4], geo_recv.at[k])
-                    column_features(geo_r[k], 2 + k)
+                    column_features(geo_r[4 * k : 4 * k + 4], 2 + k)
             build(n, chunk, at % 2)
             if at == 1:
                 if chunk >= CHUNKS // 2 and chunk % 4 == 1:
@@ -365,13 +376,16 @@
         if at == 7:
             send_spill(0, 0)
         if at == 8:
-            send_rows(3, 0)
+            send_rows(3, 4, 0)
+            send_ahead(3)
         if at == 9:
-            send_rows(2, 0)
+            send_rows(2, 3, 0)
+            send_ahead(2)
     for quarter in range(4):
         apply(ORDER[-1], quarter, 0)
-    send_rows(1, 0)
-    send_rows(0, 0)
+    send_rows(0, 2, 0)
+    send_ahead(1)
+    send_ahead(0)
 
     def spread(turn, me, count, target):
         src, dst = tile.at[turn], sums.at[turn]
@@ -398,6 +412,9 @@
             parts = [functools.reduce(jnp.add, parts[at : at + 2]) for at in range(0, len(parts), 2)]
         return parts[0]
 
+    def rows_in(low, high, it):
+        wait_for(other_in.at[it, low:high], other_recv.at[it, low])
+
     def ready(b):
         gather_block(b, 0)
         vrow[b] = two_parts(qq[b, PROBES : 2 * PROBES])
@@ -406,9 +423,12 @@
         for quarter in range(4):
             apply(n, quarter, 1)
 
+    rows_in(3, 4, 0)
     ready(3)
+    rows_in(2, 3, 0)
     ready(2)
     second(0)
+    rows_in(0, 2, 0)
     ready(1)
     ready(0)
 
@@ -416,43 +436,47 @@
         second(n)
 
     tile[...] = jnp.zeros_like(tile)
-    gram = jnp.zeros((2 * PROBES, 2 * PROBES), f32)
+    gram = jnp.zeros((6 * PROBES, 6 * PROBES), f32)
     for b in range(2):
         pair = qq[2 * c + b, 0 : 2 * PROBES]
-        gram += lax.dot_general(pair, pair, NT, precision=HIGHEST, preferred_element_type=f32)
+        parts = jnp.concatenate([piece.astype(bf16) for piece in split(pair, 3)], axis=0)
+        gram += lax.dot_general(parts, parts, NT, preferred_element_type=f32)
+    gram = gram[0:16] + gram[16:32] + gram[32:48]
+    gram = gram[:, 0:16] + gram[:, 16:32] + gram[:, 32:48]
     tile[0, :, 0:16] = gram[0:PROBES]
     tile[0, :, 16:32] = gram[PROBES:]
 
     for k in range(2):
         gather_ahead(k)
-        vnext[k] = two_parts(qn[k, PROBES:])
+        vnext[k] = two_parts(qn[1, k])
     for n in range(5, 10):
         second(n)
 
-    part = jnp.zeros((PROBES, PROBES), f32)
+    part = jnp.zeros((2 * PROBES, 2 * PROBES), f32)
     for b in range(BLOCKS):
-        part += lax.dot_general(
-            qq[b, PROBES : 2 * PROBES], tr[1, b], NT, precision=HIGHEST, preferred_element_type=f32
-        )
+        part += lax.dot_general(vrow[b], two_parts(tr[1, b]), NT, preferred_element_type=f32)
     for k in range(2):
-        part += lax.dot_general(
-            qn[k, PROBES:], tc[1, k], NT, precision=HIGHEST, preferred_element_type=f32
-        )
+        part += lax.dot_general(vnext[k], two_parts(tc[1, k]), NT, preferred_element_type=f32)
+    part = part[:PROBES] + part[PROBES:]
+    part = part[:, :PROBES] + part[:, PROBES:]
     tile[0, :, 32:40] = part * (1.0 / UNIT)
-    spread(0, inplane, plane, in_plane)
+    send(tile.at[0], sums.at[0, 0], red_send.at[0], red_recv.at[0], g, 1 - c)
+    wait_for(sums.at[0, 0], red_recv.at[0])
+    tile[1] = tile[0] + sums[0, 0]
+    spread(1, inplane, plane, in_plane)
     for k in range(2):
         send_spill(k, 1)
-    for b in range(BLOCKS):
-        send_rows(b, 1)
-    tile[1] = total_of(0, plane)
-    spread(1, place, ring, across)
-
+    send_rows(0, 4, 1)
+    tile[2] = total_of(1, plane)
+    spread(2, z, zs, along_z)
+
+    rows_in(0, 4, 1)
     for b in range(BLOCKS):
         gather_block(b, 1)
         for k in range(3 * PROBES):
             rhs[b, k] = jnp.broadcast_to(qq[b, k : k + 1], (PROBES, SLOTS))
 
-    totals = total_of(1, ring)
+    totals = total_of(2, zs)
     h00, h01, h11 = totals[:, 0:8], totals[:, 8:16], totals[:, 24:32]
     curv_inv = inverse(level * h00 + sill * h01)
     left = mm(curv_inv, totals[:, 0:40])
@@ -481,7 +505,7 @@
 
     for copy in sends:
         copy.wait_send()
-    for turn, count in enumerate((plane, ring)):
+    for turn, count in ((1, plane), (2, zs)):
         everything = sums.at[turn, pl.ds(0, count - 1)]
         pltpu.make_async_copy(everything, everything, red_send.at[turn]).wait()
 
@@ -504,9 +528,11 @@
             pltpu.SMEM((BLOCKS,), jnp.int32),
             pltpu.VMEM((3, width), f32),
             pltpu.VMEM(block, f32),
+            pltpu.VMEM((PROBES, SLOTS), f32),
+            pltpu.VMEM((PROBES, SLOTS), f32),
             pltpu.VMEM((2, PROBES, SLOTS), f32),
             pltpu.VMEM((BLOCKS, 3 * PROBES, SLOTS), f32),
-            pltpu.VMEM((2, 2 * PROBES, SLOTS), f32),
+            pltpu.VMEM((2, 2, PROBES, SLOTS), f32),
             pltpu.VMEM((BLOCKS, 1, SLOTS), f32),
             pltpu.VMEM((BLOCKS, 128, SLOTS), f32),
             pltpu.VMEM((BLOCKS, SLOTS, 128), f32),
@@ -521,24 +547,24 @@
             pltpu.VMEM((2,) + block, f32),
             pltpu.VMEM((2, 2, PROBES, SLOTS), f32),
             pltpu.VMEM((2,) + block, f32),
-            pltpu.VMEM((2,) + block, f32),
+            pltpu.VMEM((2, 2, 2, PROBES, SLOTS), f32),
             pltpu.VMEM((2, 2, PROBES, SLOTS), f32),
-            pltpu.VMEM((2, 8, 128), f32),
-            pltpu.VMEM((2, max(plane, ring), 8, 128), f32),
+            pltpu.VMEM((3, 8, 128), f32),
+            pltpu.VMEM((3, max(plane, ring), 8, 128), f32),
             pltpu.VMEM((BLOCKS, 3 * PROBES, PROBES, SLOTS), f32),
             dma((6,)),
-            dma((2,)),
-            dma((2,)),
-            dma((2,)),
-            dma((2,)),
+            dma,
+            dma,
+            dma,
+            dma,
             dma((2, BLOCKS)),
             dma((BLOCKS,)),
             dma((2, 2, 2)),
             dma((2, BLOCKS)),
-            dma((2, BLOCKS)),
+            dma((2, 2, 2)),
             dma((2, 2)),
-            dma((2,)),
-            dma((2,)),
+            dma((3,)),
+            dma((3,)),
         ],
         compiler_params=pltpu.CompilerParams(
             collective_id=0, has_side_effects=True, vmem_limit_bytes=60 << 20

time: 45.6 us -> 45.1 us (0.989); the launches traced: 45.4 us -> 44.3 us
  Pallas kernels: 43.2 us -> 42.1 us
    pallas_call x1, Pallas kernels: 43.2 us -> 42.1 us  [on_device(): pl.pallas_call(functools.partial(kernel, groups, plane), out_shape=shape,...]
where the time goes in v4:
time: 45.1 us; the launch traced here: 44.3 us
  Pallas kernels  42.1 us (93%)
  local copies, waits for them, and re-layouts  1.53 us (3%)
  between operations  0.64 us (1%)
    pallas_call x1, Pallas kernels, on_device(): pl.pallas_call(functools.partial(kernel, groups, plane), out_shape=shape,...  42.1 us
    slice x1, local copies, waits for them, and re-layouts, on_device(): return (both[:PROBES], both[PROBES:])  1.53 us

profile of v4, /device:TPU:1, one launch (start us, length us, event | category | flops | bytes accessed | tf_op | source)
XLA Modules:
  0.0 44.3 jit_solution(11803439651271596972)
XLA Ops:
  0.6 42.1 %block_cg.1 = f32[16,2048]{1,0:T(8,128)} custom-call(f32[8,2048]{1,0:T(8,128)} %rs_ref.1, f32[3,2048]{1,0:T(4,128)} %co_ref.1, s32[4]{0:T(128)} %cnt_ref.1), custom_call_target="tpu_custom_call" | custom-call | tf_op jit(solution)/shard_map/block_cg/pallas_call | solution.py:522
  42.8 1.5 %fusion = (f32[8,2048]{1,0:T(8,128)}, f32[8,2048]{1,0:T(8,128)}) fusion(f32[16,2048]{1,0:T(8,128)} %block_cg.1), kind=kLoop, calls=%fused_computation | loop fusion | bytes 262144 | tf_op jit(solution)/shard_map/slice | solution.py:574

commit v5 on v4

--- a/solution.py
+++ b/solution.py
@@ -112,6 +112,7 @@
     spill_in,
     ahead_in,
     tile,
+    flat,
     sums,
     rhs,
     local_sem,
@@ -359,14 +360,14 @@
             for k in range(2):
                 vnext[k] = two_parts(qn[0, k])
         for chunk in range(CHUNKS):
-            if at == 1 and chunk == CHUNKS // 2:
+            if at == 1 and chunk == CHUNKS - 8:
                 wait_for(geo_r, geo_recv)
                 for k in range(2):
                     column_features(geo_r[4 * k : 4 * k + 4], 2 + k)
             build(n, chunk, at % 2)
             if at == 1:
-                if chunk >= CHUNKS // 2 and chunk % 4 == 1:
-                    across_part(then, (chunk - CHUNKS // 2) // 4, (at + 1) % 2)
+                if chunk >= CHUNKS - 8 and chunk % 2 == 1:
+                    across_part(then, (chunk - CHUNKS + 8) // 2, (at + 1) % 2)
             elif chunk % 8 == 3 and then is not None:
                 across_part(then, chunk // 8, (at + 1) % 2)
             if chunk % 8 == 7 and at > 0:
@@ -388,7 +389,7 @@
     send_ahead(0)
 
     def spread(turn, me, count, target):
-        src, dst = tile.at[turn], sums.at[turn]
+        src, dst = flat.at[turn], sums.at[turn]
 
         def one(step, carry):
             pltpu.make_async_remote_copy(
@@ -444,7 +445,7 @@
     gram = gram[0:16] + gram[16:32] + gram[32:48]
     gram = gram[:, 0:16] + gram[:, 16:32] + gram[:, 32:48]
     tile[0, :, 0:16] = gram[0:PROBES]
-    tile[0, :, 16:32] = gram[PROBES:]
+    tile[0, :, 16:24] = gram[PROBES:, PROBES:]
 
     for k in range(2):
         gather_ahead(k)
@@ -459,15 +460,18 @@
         part += lax.dot_general(vnext[k], two_parts(tc[1, k]), NT, preferred_element_type=f32)
     part = part[:PROBES] + part[PROBES:]
     part = part[:, :PROBES] + part[:, PROBES:]
-    tile[0, :, 32:40] = part * (1.0 / UNIT)
-    send(tile.at[0], sums.at[0, 0], red_send.at[0], red_recv.at[0], g, 1 - c)
+    tile[0, :, 24:32] = part * (1.0 / UNIT)
+    for i in range(PROBES):
+        wide = slice(32 * (i % 4), 32 * (i % 4) + 32)
+        flat[0, i // 4 : i // 4 + 1, wide] = tile[0, i : i + 1, 0:32]
+    send(flat.at[0], sums.at[0, 0], red_send.at[0], red_recv.at[0], g, 1 - c)
     wait_for(sums.at[0, 0], red_recv.at[0])
-    tile[1] = tile[0] + sums[0, 0]
+    flat[1] = flat[0] + sums[0, 0]
     spread(1, inplane, plane, in_plane)
     for k in range(2):
         send_spill(k, 1)
     send_rows(0, 4, 1)
-    tile[2] = total_of(1, plane)
+    flat[2] = total_of(1, plane)
     spread(2, z, zs, along_z)
 
     rows_in(0, 4, 1)
@@ -476,11 +480,15 @@
         for k in range(3 * PROBES):
             rhs[b, k] = jnp.broadcast_to(qq[b, k : k + 1], (PROBES, SLOTS))
 
-    totals = total_of(2, zs)
-    h00, h01, h11 = totals[:, 0:8], totals[:, 8:16], totals[:, 24:32]
+    flat[3] = total_of(2, zs)
+    for i in range(PROBES):
+        wide = slice(32 * (i % 4), 32 * (i % 4) + 32)
+        tile[0, i : i + 1, 0:32] = flat[3, i // 4 : i // 4 + 1, wide]
+    totals = tile[0, :, 0:32]
+    h00, h01, h11 = totals[:, 0:8], totals[:, 8:16], totals[:, 16:24]
     curv_inv = inverse(level * h00 + sill * h01)
-    left = mm(curv_inv, totals[:, 0:40])
-    alpha, m2, m1, m12 = (left[:, at : at + PROBES] for at in (0, 8, 24, 32))
+    left = mm(curv_inv, totals)
+    alpha, m2, m1, m12 = (left[:, at : at + PROBES] for at in (0, 8, 16, 24))
     alpha_t = mm(h00, curv_inv)
     w_t = sill * mm(h01, curv_inv)
     middle = mm(h01, m2)
@@ -549,8 +557,9 @@
             pltpu.VMEM((2,) + block, f32),
             pltpu.VMEM((2, 2, 2, PROBES, SLOTS), f32),
             pltpu.VMEM((2, 2, PROBES, SLOTS), f32),
-            pltpu.VMEM((3, 8, 128), f32),
-            pltpu.VMEM((3, max(plane, ring), 8, 128), f32),
+            pltpu.VMEM((1, 8, 128), f32),
+            pltpu.VMEM((4, 2, 128), f32),
+            pltpu.VMEM((3, max(plane, ring), 2, 128), f32),
             pltpu.VMEM((BLOCKS, 3 * PROBES, PROBES, SLOTS), f32),
             dma((6,)),
             dma,

time: 45.1 us -> 44.6 us (0.989)
  no operation moved by 1% of the time
where the time goes in v5:
time: 44.6 us; the launch traced here: 44 us
  Pallas kernels  41.9 us (94%)
  local copies, waits for them, and re-layouts  1.53 us (3%)
  between operations  0.64 us (1%)
    pallas_call x1, Pallas kernels, on_device(): pl.pallas_call(functools.partial(kernel, groups, plane), out_shape=shape,...  41.9 us
    slice x1, local copies, waits for them, and re-layouts, on_device(): return (both[:PROBES], both[PROBES:])  1.53 us

profile of v5, /device:TPU:1, one launch (start us, length us, event | category | flops | bytes accessed | tf_op | source)
XLA Modules:
  0.0 44.0 jit_solution(11308482443527227644)
XLA Ops:
  0.6 41.9 %block_cg.1 = f32[16,2048]{1,0:T(8,128)} custom-call(f32[8,2048]{1,0:T(8,128)} %rs_ref.1, f32[3,2048]{1,0:T(4,128)} %co_ref.1, s32[4]{0:T(128)} %cnt_ref.1), custom_call_target="tpu_custom_call" | custom-call | tf_op jit(solution)/shard_map/block_cg/pallas_call | solution.py:530
  42.5 1.5 %fusion = (f32[8,2048]{1,0:T(8,128)}, f32[8,2048]{1,0:T(8,128)}) fusion(f32[16,2048]{1,0:T(8,128)} %block_cg.1), kind=kLoop, calls=%fused_computation | loop fusion | bytes 262144 | tf_op jit(solution)/shard_map/slice | solution.py:583
